TPU v7x, 256 devices: a whole 4x4x8 slice. The times are simulated.
256 devices in a mesh: seq: 64 (over z, y, core), dp: 4 (over x).
Axes of the slice: x: 4, y: 4, z: 8, core: 2. Of those that a mesh axis runs over, the one named last changes fastest.
Arguments:
- queries: bfloat16 [4, 32768, 1024], P('dp', 'seq'), may hold values from -8 to 8
- memory_keys: bfloat16 [4, 32768, 1024], P('dp', 'seq'), may hold values from -8 to 8
- memory_values: bfloat16 [4, 32768, 1024], P('dp', 'seq'), may hold values from -6 to 6
- out_weight: bfloat16 [1024, 2048], P('seq'), may hold values from -0.1875 to 0.1875
- grad_out: bfloat16 [4, 32768, 2048], P('dp', 'seq'), may hold values from -6 to 6
- key_first: int32 [4, 256], P('dp', 'seq'), may hold values from 0 to 254, as said below
- key_last: int32 [4, 256], P('dp', 'seq'), may hold values from 2 to 256
Outputs:
- layer_out: bfloat16 [4, 32768, 2048], P('dp', 'seq')
- grad_query: bfloat16 [4, 32768, 1024], P('dp', 'seq')
- grad_keys: bfloat16 [4, 32768, 1024], P('dp', 'seq')
- grad_values: bfloat16 [4, 32768, 1024], P('dp', 'seq')
- weight_grad: float32 [1024, 2048], P('seq')
Inputs may be any that keep to these rules, and one draw needn't show every extreme that they name: With key_last: query block b of pack p attends to key blocks key_first[p, b] to key_last[p, b] - 1, blocks of 128 tokens. Sentence pairs tile aligned groups of 4 blocks that begin at block 2, the first and last groups holding 4 // 2 blocks; a query block's key blocks lie in its own group and number 1 to 3, 3 in some group of every pack.
All inputs are finite; a program needn't handle non-finite values.
Results may differ from a plain program's by a relative error of at most 0.0095.
Values may be sent and summed in bfloat16 or wider, within the bound.
A program may use at most 192 MiB of HBM per device.

v0:
```python
import math
import jax
import jax.numpy as jnp
from jax import lax
from jax.sharding import PartitionSpec as P

HDIM = 128
HEADS = 8
BLOCK = 128
REACH = 256


def padded_2(block, sides, width):
    for axis, dim in sides:
        count = lax.axis_size(axis)
        forward = [(i, i + 1) for i in range(count - 1)]
        backward = [(target, source) for source, target in forward]
        low = lax.ppermute(
            lax.slice_in_dim(block, block.shape[dim] - width, None, axis=dim), axis, forward
        )
        high = lax.ppermute(lax.slice_in_dim(block, 0, width, axis=dim), axis, backward)
        block = jnp.concatenate([low, block, high], axis=dim)
    return block


def passed_along(block, axis, distance):
    devices = range(lax.axis_size(axis))
    route = [(i - distance, i) for i in devices if i - distance in devices]
    return lax.ppermute(block, axis, route)


def run_tiles(
    query_rows, grad_rows, kv_source, window_starts, window_rows, lower, upper, row_anchor
):
    rows_dev, width_hd = query_rows.shape
    set_count = rows_dev // BLOCK // 4
    score_scale = 1.0 / math.sqrt(HDIM)

    def advance(running, set_index):
        member_ids = set_index * 4 + jnp.arange(4, dtype=jnp.int32)
        query_set = query_rows.reshape(4, BLOCK, HEADS, HDIM)
        grad_set = grad_rows.reshape(4, BLOCK, HEADS, HDIM)
        starts = window_starts[member_ids]
        kv_tiles = jax.vmap(
            lambda offset: lax.dynamic_slice_in_dim(kv_source, offset, window_rows, 1)
        )(starts)
        key_tiles = kv_tiles[:, 0].reshape(4, window_rows, HEADS, HDIM)
        value_tiles = kv_tiles[:, 1].reshape(4, window_rows, HEADS, HDIM)
        positions = (
            row_anchor + starts[:, None] + jnp.arange(window_rows, dtype=jnp.int32)[None, :]
        ) // BLOCK
        allowed = (positions >= lower[member_ids][:, None]) & (
            positions < upper[member_ids][:, None]
        )
        inside = allowed[:, None, None, :]
        scores = (
            jnp.einsum("jqhd,jkhd->jhqk", query_set, key_tiles, preferred_element_type=jnp.float32)
            * score_scale
        )
        highest = jnp.max(jnp.where(inside, scores, -jnp.inf), axis=-1, keepdims=True)
        raised = jnp.where(inside, jnp.exp(scores - highest), 0.0)
        softmax_probs = raised / jnp.sum(raised, axis=-1, keepdims=True)
        weights = softmax_probs.astype(jnp.bfloat16)
        attended = jnp.einsum(
            "jhqk,jkhd->jqhd", weights, value_tiles, preferred_element_type=jnp.float32
        ).astype(jnp.bfloat16)
        grad_probs = jnp.einsum(
            "jqhd,jkhd->jhqk", grad_set, value_tiles, preferred_element_type=jnp.float32
        )
        row_term = jnp.sum(softmax_probs * grad_probs, axis=-1, keepdims=True)
        grad_scores = (softmax_probs * (grad_probs - row_term) * score_scale).astype(jnp.bfloat16)
        grad_query = jnp.einsum(
            "jhqk,jkhd->jqhd", grad_scores, key_tiles, preferred_element_type=jnp.float32
        ).astype(jnp.bfloat16)
        key_part = jnp.einsum(
            "jhqk,jqhd->jkhd", grad_scores, query_set, preferred_element_type=jnp.float32
        ).reshape(4, window_rows, width_hd)
        value_part = jnp.einsum(
            "jhqk,jqhd->jkhd", weights, grad_set, preferred_element_type=jnp.float32
        ).reshape(4, window_rows, width_hd)
        contributions = jnp.stack([key_part, value_part], axis=1)
        for member in range(4):
            offset = starts[member]
            current = lax.dynamic_slice_in_dim(running, offset, window_rows, 1)
            running = lax.dynamic_update_slice_in_dim(
                running, current + contributions[member], offset, 1
            )
        return (
            running,
            (attended.reshape(4 * BLOCK, width_hd), grad_query.reshape(4 * BLOCK, width_hd)),
        )

    empty_sum = jnp.zeros((2, kv_source.shape[1], width_hd), jnp.float32)
    grad_sums, outputs = lax.scan(advance, empty_sum, jnp.arange(set_count, dtype=jnp.int32))
    return (
        grad_sums,
        outputs[0].reshape(rows_dev, width_hd),
        outputs[1].reshape(rows_dev, width_hd),
    )


def body(queries, memory_keys, memory_values, out_weight, grad_out, key_first, key_last):
    query_rows = queries[0]
    dy_rows = grad_out[0]
    first_blocks = key_first[0]
    last_blocks = key_last[0]
    rows_dev, width_hd = query_rows.shape
    block_count = rows_dev // BLOCK
    window_rows = BLOCK + 2 * REACH
    whole_weight = lax.all_gather(out_weight, "seq", axis=0, tiled=True)
    grad_attn = lax.dot_general(
        dy_rows, whole_weight, (((1,), (1,)), ((), ())), preferred_element_type=jnp.float32
    ).astype(jnp.bfloat16)
    stacked = jnp.stack([memory_keys[0], memory_values[0]])
    padded = padded_2(stacked, (("seq", 1),), REACH)
    halo_anchor = lax.axis_index("seq") * rows_dev - REACH
    window_starts = jnp.arange(block_count, dtype=jnp.int32) * BLOCK
    grad_sums, attended, grad_query = run_tiles(
        query_rows,
        grad_attn,
        padded,
        window_starts,
        window_rows,
        first_blocks,
        last_blocks,
        halo_anchor,
    )
    left_rim = grad_sums[:, :REACH]
    right_rim = grad_sums[:, REACH + rows_dev :]
    from_right = passed_along(left_rim.astype(jnp.bfloat16), "seq", -1).astype(left_rim.dtype)
    from_left = passed_along(right_rim.astype(jnp.bfloat16), "seq", 1).astype(right_rim.dtype)
    own_sums = grad_sums[:, REACH : REACH + rows_dev]
    own_sums = own_sums.at[:, :REACH].add(from_left)
    own_sums = own_sums.at[:, rows_dev - REACH :].add(from_right)
    key_grad = own_sums[0].astype(jnp.bfloat16)
    value_grad = own_sums[1].astype(jnp.bfloat16)
    layer_out = jnp.dot(attended, whole_weight, preferred_element_type=jnp.float32).astype(
        jnp.bfloat16
    )
    normalizer = math.sqrt(lax.axis_size("seq") * rows_dev)
    shard_sum = lax.psum_scatter(
        lax.dot_general(
            attended, dy_rows, (((0,), (0,)), ((), ())), preferred_element_type=jnp.float32
        ),
        "seq",
        scatter_dimension=0,
        tiled=True,
    )
    summed = lax.psum(shard_sum.astype(jnp.bfloat16), "dp").astype(jnp.float32)
    weight_grad = summed / normalizer
    return (layer_out[None], grad_query[None], key_grad[None], value_grad[None], weight_grad)


def solution(mesh):
    return jax.shard_map(
        body,
        mesh=mesh,
        in_specs=(
            P("dp", "seq", None),
            P("dp", "seq", None),
            P("dp", "seq", None),
            P("seq", None),
            P("dp", "seq", None),
            P("dp", "seq"),
            P("dp", "seq"),
        ),
        out_specs=(
            P("dp", "seq", None),
            P("dp", "seq", None),
            P("dp", "seq", None),
            P("dp", "seq", None),
            P("seq", None),
        ),
        check_vma=False,
    )
```

profile of v0, /device:TPU:8, one launch (start us, length us, event | category | flops | bytes accessed | tf_op | source)
XLA Modules:
  0.0 405.0 jit_solution(8110936625988158264)
XLA Ops:
  13.4 1.9 collective-permute-start.1
  15.3 2.4 collective-permute-start
  19.8 1.5 copy.54
  22.9 5.4 %collective-permute-done.1 = bf16[2,256,1024]{2,1,0:T(8,128)(2,1)} collective-permute-done((bf16[2,256,1024]{2,1,0:T(8,128)(2,1)}, bf16[2,256,1024]{2,1,0:T(8,128)(2,1)}, u32[]{:S(2)}, u32[]{:S(2)}) %collective-permute-start.1) | collective-permute-done | bytes 1048608 | tf_op jit(solution)/shard_map/ppermute | solution.py:21
  28.3 4.4 %collective-permute-done = bf16[2,256,1024]{2,1,0:T(8,128)(2,1)} collective-permute-done((bf16[2,256,1024]{2,1,0:T(8,128)(2,1)}, bf16[2,256,1024]{2,1,0:T(8,128)(2,1)}, u32[]{:S(2)}, u32[]{:S(2)}) %collective-permute-start) | collective-permute-done | bytes 1048608 | tf_op jit(solution)/shard_map/ppermute | solution.py:18
  32.7 3.8 pad_maximum_fusion.1
  36.5 21.0 %while.3 = (s32[]{:T(128)}, bf16[2,1024,1024]{2,1,0:T(8,128)(2,1)}, s32[4,3]{1,0:T(4,128)S(1)}, bf16[4,2,640,1024]{3,2,1,0:T(8,128)(2,1)}, s32[]{:T(128)}) while((s32[]{:T(128)}, bf16[2,1024,1024]{2,1,0:T(8,128)(2,1)}, s32[4,3]{1,0:T(4,128)S(1)}, bf16[4,2,640,1024]{3,2,1,0:T(8,128)(2,1)}, s32[]{:T(128)}) %tuple.39), condition=%wide.while_cond.2, body=%wide.while_body.2.sunk | while | flops 2 | bytes 5243501 | solution.py:45
  37.0 4.7 %bitcast_dynamic-update-slice_fusion.2 = bf16[4,2,640,1024]{3,2,1,0:T(8,128)(2,1)} fusion(bf16[4,2,640,1024]{3,2,1,0:T(8,128)(2,1)} %get-tuple-element.131, s32[]{:T(128)S(6)} %copy.69, bf16[2,1024,1024]{2,1,0:T(8,128)(2,1)} %get-tuple-element.134, s32[]{:T(128)} %bitcast.105), kind=kLoop, calls=%fused_computation.3.clone.1 | loop fusion | bytes 5243396 | tf_op jit(solution)/shard_map/while/body/eval_jaxpr/vmap()/gather
  42.3 4.6 %bitcast_dynamic-update-slice_fusion.2 = bf16[4,2,640,1024]{3,2,1,0:T(8,128)(2,1)} fusion(bf16[4,2,640,1024]{3,2,1,0:T(8,128)(2,1)} %get-tuple-element.131, s32[]{:T(128)S(6)} %copy.69, bf16[2,1024,1024]{2,1,0:T(8,128)(2,1)} %get-tuple-element.134, s32[]{:T(128)} %bitcast.105), kind=kLoop, calls=%fused_computation.3.clone.1 | loop fusion | bytes 5243396 | tf_op jit(solution)/shard_map/while/body/eval_jaxpr/vmap()/gather
  47.5 4.6 %bitcast_dynamic-update-slice_fusion.2 = bf16[4,2,640,1024]{3,2,1,0:T(8,128)(2,1)} fusion(bf16[4,2,640,1024]{3,2,1,0:T(8,128)(2,1)} %get-tuple-element.131, s32[]{:T(128)S(6)} %copy.69, bf16[2,1024,1024]{2,1,0:T(8,128)(2,1)} %get-tuple-element.134, s32[]{:T(128)} %bitcast.105), kind=kLoop, calls=%fused_computation.3.clone.1 | loop fusion | bytes 5243396 | tf_op jit(solution)/shard_map/while/body/eval_jaxpr/vmap()/gather
  52.7 4.7 %bitcast_dynamic-update-slice_fusion.2 = bf16[4,2,640,1024]{3,2,1,0:T(8,128)(2,1)} fusion(bf16[4,2,640,1024]{3,2,1,0:T(8,128)(2,1)} %get-tuple-element.131, s32[]{:T(128)S(6)} %copy.69, bf16[2,1024,1024]{2,1,0:T(8,128)(2,1)} %get-tuple-element.134, s32[]{:T(128)} %bitcast.105), kind=kLoop, calls=%fused_computation.3.clone.1 | loop fusion | bytes 5243396 | tf_op jit(solution)/shard_map/while/body/eval_jaxpr/vmap()/gather
  57.4 5.4 %slice.116 = bf16[4,1,640,1024]{3,2,1,0:T(8,128)(2,1)} slice(bf16[4,2,640,1024]{3,2,1,0:T(8,128)(2,1)} %get-tuple-element.69), slice={[0:4], [1:2], [0:640], [0:1024]} | slice | bytes 10485760 | tf_op jit(solution)/shard_map/while/body/eval_jaxpr/slice | solution.py:48
  62.9 15.4 %copy.30 = bf16[4,2,640,1024]{2,3,0,1:T(8,128)(2,1)} copy(bf16[4,2,640,1024]{3,2,1,0:T(8,128)(2,1)} %get-tuple-element.69) | data formatting | bytes 20971520 | tf_op jit(solution)/shard_map/while/body/eval_jaxpr/vmap()/gather | solution.py:45
  78.2 8.0 %copy.29 = bf16[4,1,640,1024]{2,3,0,1:T(8,128)(2,1)} copy(bf16[4,1,640,1024]{3,2,1,0:T(8,128)(2,1)} %slice.116) | data formatting | bytes 10485760 | tf_op jit(solution)/shard_map/while/body/eval_jaxpr/slice | solution.py:48
  86.2 5.3 %slice.156 = bf16[4,1,640,1024]{2,3,0,1:T(8,128)(2,1)} slice(bf16[4,2,640,1024]{2,3,0,1:T(8,128)(2,1)} %copy.30), slice={[0:4], [0:1], [0:640], [0:1024]} | slice | bytes 10485760 | tf_op jit(solution)/shard_map/while/body/eval_jaxpr/slice | solution.py:47
  91.6 14.1 %bitcast_reduce_fusion = (f32[4,8,128]{2,1,0:T(8,128)S(1)}, f32[4,8,640,128]{3,2,1,0:T(8,128)}) fusion(pred[4,640]{1,0:T(4,128)(4,1)S(1)} %compare_and_fusion, bf16[4,640,8,128]{1,3,2,0:T(8,128)(2,1)} %bitcast.112, bf16[4,128,8,128]{1,3,2,0:T(8,128)(2,1)S(1)} %copy-done.6), kind=kOutput, calls=%fused_computation.14 | convolution fusion | flops 1357906560 | bytes 16796160 | tf_op jit(solution)/shard_map/while/body/eval_jaxpr/sub | solution.py:61
  105.7 8.1 %fusion.50 = bf16[4,128,8,128]{1,3,2,0:T(8,128)(2,1)} fusion(bf16[4,640,8,128]{1,3,2,0:T(8,128)(2,1)} %bitcast.108, f32[4,8,640,128]{3,2,1,0:T(8,128)} %get-tuple-element.97, f32[4,8,128]{2,1,0:T(8,128)S(1)} %get-tuple-element.96), kind=kOutput, calls=%fused_computation.58 | convolution fusion | flops 676855808 | bytes 16793600 | tf_op jit(solution)/shard_map/while/body/eval_jaxpr/jhqk,jkhd->jqhd/dot_general | solution.py:64
  113.8 2.4 copy.34
  116.2 7.0 %fusion.37 = f32[1024,2048]{1,0:T(8,128)} fusion(bf16[1,512,2048]{2,1,0:T(8,128)(2,1)S(1)} %copy-done, bf16[64,8,8,128]{3,2,1,0:T(8,128)(2,1)} %bitcast.117), kind=kOutput, calls=%fused_computation.51 | convolution fusion | flops 2147483648 | bytes 11534336 | tf_op jit(solution)/shard_map/dot_general | solution.py:142
  131.8 4.5 %fusion.56 = bf16[64,8,8,128]{3,1,2,0:T(8,128)(2,1)S(1)} fusion(bf16[1024,2048]{1,0:T(8,128)(2,1)} %all-gather.2.cloned.1.call-done, bf16[1,512,2048]{2,1,0:T(8,128)(2,1)S(1)} %copy-done), kind=kOutput, calls=%fused_computation.60 | convolution fusion | flops 2148007936 | bytes 7340032 | tf_op jit(solution)/shard_map/dot_general | solution.py:111
  137.4 7.9 %fusion.78 = f32[4,8,128,640]{2,3,1,0:T(8,128)} fusion(bf16[4,128,8,128]{1,3,2,0:T(8,128)(2,1)S(1)} %copy.43, bf16[4,640,8,128]{1,3,2,0:T(8,128)(2,1)} %bitcast.109), kind=kOutput, calls=%fused_computation.94 | convolution fusion | flops 671088640 | bytes 16777216 | tf_op jit(solution)/shard_map/while/body/eval_jaxpr/jqhd,jkhd->jhqk/dot_general | solution.py:67
  145.3 18.9 %fusion.10 = f32[4,8,640,128]{2,3,1,0:T(8,128)} fusion(bf16[4,128,8,128]{1,3,2,0:T(8,128)(2,1)S(1)} %copy-done.6, f32[4,8,128,640]{2,3,1,0:T(8,128)} %fusion.78, f32[4,8,640,128]{3,2,1,0:T(8,128)} %get-tuple-element.97, f32[4,8,128]{2,1,0:T(8,128)S(1)} %get-tuple-element.96), kind=kOutput, calls=%fused_computation.22 | convolution fusion | flops 689443456 | bytes 32522240 | tf_op jit(solution)/shard_map/while/body/eval_jaxpr/jhqk,jqhd->jkhd/dot_general | solution.py:75
  164.2 11.4 %copy.45 = f32[4,1,640,1024]{3,2,1,0:T(8,128)} copy(f32[4,1,640,1024]{2,3,0,1:T(8,128)} %bitcast.110) | data formatting | bytes 20971520 | tf_op jit(solution)/shard_map/while/body/eval_jaxpr/stack;while/body/eval_jaxpr/reshape | solution.py:81
  175.6 10.2 %fusion.31 = f32[4,8,128,640]{3,2,1,0:T(8,128)} fusion(bf16[4,128,8,128]{1,3,2,0:T(8,128)(2,1)S(1)} %copy.43, f32[4,8,640,128]{3,2,1,0:T(8,128)} %get-tuple-element.97, f32[4,8,128]{2,1,0:T(8,128)S(1)} %get-tuple-element.96), kind=kOutput, calls=%fused_computation.43 | convolution fusion | flops 676331520 | bytes 22036480 | tf_op jit(solution)/shard_map/while/body/eval_jaxpr/jhqk,jqhd->jkhd/dot_general | solution.py:78
  185.8 11.4 %copy.46 = f32[4,1,640,1024]{3,2,1,0:T(8,128)} copy(f32[4,1,640,1024]{2,3,0,1:T(8,128)} %bitcast.111) | data formatting | bytes 20971520 | tf_op jit(solution)/shard_map/while/body/eval_jaxpr/stack;while/body/eval_jaxpr/reshape | solution.py:81
  197.2 5.7 %fusion.19 = f32[2,640,1024]{2,1,0:T(8,128)} fusion(f32[4,1,640,1024]{3,2,1,0:T(8,128)} %copy.45, f32[4,1,640,1024]{3,2,1,0:T(8,128)} %copy.46), kind=kLoop, calls=%fused_computation.28 | loop fusion | flops 1310720 | bytes 26214400 | tf_op jit(solution)/shard_map/while/body/eval_jaxpr/squeeze | solution.py:86
  202.9 4.3 %broadcast_in_dim.65 = f32[2,1024,1024]{2,1,0:T(8,128)} broadcast(f32[]{:T(128)} %constant.118.clone.1), dimensions={} | broadcast | bytes 8388612 | tf_op jit(solution)/shard_map/broadcast_in_dim | solution.py:93
  207.2 15.0 %dynamic_update_slice.21 = f32[2,1024,1024]{2,1,0:T(8,128)} dynamic-update-slice(f32[2,1024,1024]{2,1,0:T(8,128)} %broadcast_in_dim.65, f32[2,640,1024]{2,1,0:T(8,128)} %fusion.19, s32[]{:T(128)} %constant.105.clone.1, s32[]{:T(128)S(6)} %select_n.64, s32[]{:T(128)} %constant.105.clone.1) | dynamic-update-slice | bytes 10485764 | tf_op jit(solution)/shard_map/while/body/eval_jaxpr/dynamic_update_slice | solution.py:85
  222.2 8.5 %fusion.22 = f32[2,640,1024]{2,1,0:T(8,128)} fusion(f32[4,1,640,1024]{3,2,1,0:T(8,128)} %copy.45, f32[4,1,640,1024]{3,2,1,0:T(8,128)} %copy.46, f32[2,1024,1024]{2,1,0:T(8,128)} %dynamic_update_slice.21, s32[]{:T(128)S(6)} %select_n.65), kind=kLoop, calls=%fused_computation.31 | loop fusion | flops 2621440 | bytes 31457284 | tf_op jit(solution)/shard_map/while/body/eval_jaxpr/add | solution.py:86
  230.7 15.0 %dynamic_update_slice.22 = f32[2,1024,1024]{2,1,0:T(8,128)} dynamic-update-slice(f32[2,1024,1024]{2,1,0:T(8,128)} %dynamic_update_slice.21, f32[2,640,1024]{2,1,0:T(8,128)} %fusion.22, s32[]{:T(128)} %constant.105.clone.1, s32[]{:T(128)S(6)} %select_n.65, s32[]{:T(128)} %constant.105.clone.1) | dynamic-update-slice | bytes 10485764 | tf_op jit(solution)/shard_map/while/body/eval_jaxpr/dynamic_update_slice | solution.py:85
  245.6 8.3 %fusion.17 = f32[2,640,1024]{2,1,0:T(8,128)} fusion(f32[4,1,640,1024]{3,2,1,0:T(8,128)} %copy.45, f32[4,1,640,1024]{3,2,1,0:T(8,128)} %copy.46, f32[2,1024,1024]{2,1,0:T(8,128)} %dynamic_update_slice.22, s32[]{:T(128)S(6)} %select_n.66), kind=kLoop, calls=%fused_computation.26 | loop fusion | flops 2621440 | bytes 31457284 | tf_op jit(solution)/shard_map/while/body/eval_jaxpr/add | solution.py:86
  253.9 14.9 %dynamic_update_slice.23 = f32[2,1024,1024]{2,1,0:T(8,128)} dynamic-update-slice(f32[2,1024,1024]{2,1,0:T(8,128)} %dynamic_update_slice.22, f32[2,640,1024]{2,1,0:T(8,128)} %fusion.17, s32[]{:T(128)} %constant.105.clone.1, s32[]{:T(128)S(6)} %select_n.66, s32[]{:T(128)} %constant.105.clone.1) | dynamic-update-slice | bytes 10485764 | tf_op jit(solution)/shard_map/while/body/eval_jaxpr/dynamic_update_slice | solution.py:85
  268.8 8.3 %fusion.24 = f32[2,640,1024]{2,1,0:T(8,128)} fusion(f32[4,1,640,1024]{3,2,1,0:T(8,128)} %copy.46, f32[4,1,640,1024]{3,2,1,0:T(8,128)} %copy.45, f32[2,1024,1024]{2,1,0:T(8,128)} %dynamic_update_slice.23, s32[]{:T(128)S(6)} %select_n.67), kind=kLoop, calls=%fused_computation.34 | loop fusion | flops 2621440 | bytes 31457284 | tf_op jit(solution)/shard_map/while/body/eval_jaxpr/add | solution.py:86
  277.0 14.3 %dynamic_update_slice.24 = f32[2,1024,1024]{2,1,0:T(8,128)} dynamic-update-slice(f32[2,1024,1024]{2,1,0:T(8,128)} %dynamic_update_slice.23, f32[2,640,1024]{2,1,0:T(8,128)} %fusion.24, s32[]{:T(128)} %constant.105.clone.1, s32[]{:T(128)S(6)} %select_n.67, s32[]{:T(128)} %constant.105.clone.1) | dynamic-update-slice | bytes 10485764 | tf_op jit(solution)/shard_map/while/body/eval_jaxpr/dynamic_update_slice | solution.py:85
  291.3 4.0 convert.8
  295.4 1.5 fusion.74
  296.9 1.9 collective-permute-start.2
  298.8 3.6 collective-permute-start.3
  302.5 19.4 %fusion.53 = bf16[4,128,8,128]{1,3,2,0:T(8,128)(2,1)} fusion(bf16[4,640,8,128]{1,3,2,0:T(8,128)(2,1)} %bitcast.113, f32[4,8,128,640]{2,3,1,0:T(8,128)} %fusion.78, f32[4,8,640,128]{3,2,1,0:T(8,128)} %get-tuple-element.97, f32[4,8,128]{2,1,0:T(8,128)S(1)} %get-tuple-element.96), kind=kOutput, calls=%fused_computation.59 | convolution fusion | flops 689967744 | bytes 27279360 | tf_op jit(solution)/shard_map/while/body/eval_jaxpr/jhqk,jkhd->jqhd/dot_general | solution.py:72
  321.9 5.0 %slice.163 = f32[2,512,1024]{2,1,0:T(8,128)} slice(f32[2,1024,1024]{2,1,0:T(8,128)} %dynamic_update_slice.24), slice={[0:2], [256:768], [0:1024]} | slice | bytes 8388608 | tf_op jit(solution)/shard_map/slice | solution.py:132
  326.9 1.7 copy.40
  329.8 6.0 %fusion.30 = bf16[1,512,2048]{2,1,0:T(8,128)(2,1)} fusion(bf16[1024,2048]{1,0:T(8,128)(2,1)} %all-gather.2.cloned.1.call-done, bf16[64,8,8,128]{3,2,1,0:T(8,128)(2,1)S(1)} %bitcast.118), kind=kOutput, calls=%fused_computation.42 | convolution fusion | flops 2148532224 | bytes 7340032 | tf_op jit(solution)/shard_map/dot_general | solution.py:137
  335.8 2.3 fusion.36
  338.7 1.7 convert.9
  340.4 1.5 convert_element_type.56
  342.0 3.0 fusion.75
  345.0 51.9 %all-reduce.2.cloned.1.call-done = bf16[16,2048]{1,0:T(8,128)(2,1)} async-done(((bf16[16,2048]{1,0:T(8,128)(2,1)}), bf16[16,2048]{1,0:T(8,128)(2,1)}) %all-reduce.2.cloned.1.call-update) | async-done | bytes 65552 | tf_op jit(solution)/shard_map/psum | solution.py:149
  396.9 1.5 convert_multiply_fusion
  (56 shorter events, 15.9 us)
Async XLA Ops:
  7.2 109.0 %copy-start = (bf16[1,512,2048]{2,1,0:T(8,128)(2,1)S(1)}, bf16[1,512,2048]{2,1,0:T(8,128)(2,1)}, u32[]{:S(2)}) copy-start(bf16[1,512,2048]{2,1,0:T(8,128)(2,1)} %param.15) | copy-start | bytes 6291460
  7.2 11.3 %copy-start.2 = (s32[1,4]{1,0:T(1,128)S(1)}, s32[1,4]{1,0:T(1,128)}, u32[]{:S(2)}) copy-start(s32[1,4]{1,0:T(1,128)} %param.17) | copy-start | bytes 52
  7.2 12.0 %copy-start.3 = (s32[1,4]{1,0:T(1,128)S(1)}, s32[1,4]{1,0:T(1,128)}, u32[]{:S(2)}) copy-start(s32[1,4]{1,0:T(1,128)} %param.16) | copy-start | bytes 52
  7.2 124.5 %all-gather.2.cloned.1.call-start = ((), (), s32[]{:S(2)}) async-start(), calls=%async_computation.1 | async-start | bytes 4259840 | tf_op jit(solution)/shard_map/all_gather | solution.py:110
  7.9 332.5 %reduce-scatter.2.cloned.1.call-start = ((), (), s32[]{:S(2)}) async-start(), calls=%async_computation.2 | async-start | bytes 8519680 | tf_op jit(solution)/shard_map/reduce_scatter | solution.py:141
  10.6 1.3 copy-start.5
  13.4 14.9 %collective-permute-start.1 = (bf16[2,256,1024]{2,1,0:T(8,128)(2,1)}, bf16[2,256,1024]{2,1,0:T(8,128)(2,1)}, u32[]{:S(2)}, u32[]{:S(2)}) collective-permute-start(bf16[2,256,1024]{2,1,0:T(8,128)(2,1)} %get-tuple-element.91), channel_id=1, source_target_pairs={{4,0},{8,4},{12,8},{16,12},{20,16},{24,20},{28,24},{32,28},{36,32}... | collective-permute-start | bytes 3145736 | tf_op jit(solution)/shard_map/ppermute | solution.py:21
  15.3 17.4 %collective-permute-start = (bf16[2,256,1024]{2,1,0:T(8,128)(2,1)}, bf16[2,256,1024]{2,1,0:T(8,128)(2,1)}, u32[]{:S(2)}, u32[]{:S(2)}) collective-permute-start(bf16[2,256,1024]{2,1,0:T(8,128)(2,1)} %get-tuple-element.90), channel_id=1, source_target_pairs={{0,4},{4,8},{8,12},{12,16},{16,20},{20,24},{24,28},{28,32},{32,36}... | collective-permute-start | bytes 3145736 | tf_op jit(solution)/shard_map/ppermute | solution.py:18
  78.2 13.3 %copy-start.6 = (bf16[4,128,8,128]{1,3,2,0:T(8,128)(2,1)S(1)}, bf16[4,128,8,128]{1,3,2,0:T(8,128)(2,1)}, u32[]{:S(2)}) copy-start(bf16[4,128,8,128]{1,3,2,0:T(8,128)(2,1)} %copy.42) | copy-start | bytes 3145732
  123.1 273.8 %all-reduce.2.cloned.1.call-start = ((), (), s32[]{:S(2)}) async-start(), calls=%async_computation.3 | async-start | bytes 131072 | tf_op jit(solution)/shard_map/psum | solution.py:149
  296.9 38.9 %collective-permute-start.2 = (bf16[2,256,1024]{2,1,0:T(8,128)(2,1)}, bf16[2,256,1024]{2,1,0:T(8,128)(2,1)}, u32[]{:S(2)}, u32[]{:S(2)}) collective-permute-start(bf16[2,256,1024]{2,1,0:T(8,128)(2,1)} %get-tuple-element.87), channel_id=1, source_target_pairs={{0,4},{4,8},{8,12},{12,16},{16,20},{20,24},{24,28},{28,32},{32,36}... | collective-permute-start | bytes 3145736 | tf_op jit(solution)/shard_map/ppermute | solution.py:29
  298.8 39.3 %collective-permute-start.3 = (bf16[2,256,1024]{2,1,0:T(8,128)(2,1)}, bf16[2,256,1024]{2,1,0:T(8,128)(2,1)S(1)}, u32[]{:S(2)}, u32[]{:S(2)}) collective-permute-start(bf16[2,256,1024]{2,1,0:T(8,128)(2,1)} %get-tuple-element.86), channel_id=1, source_target_pairs={{4,0},{8,4},{12,8},{16,12},{20,16},{24,20},{28,24},{32,28},{36,32}... | collective-permute-start | bytes 3145736 | tf_op jit(solution)/shard_map/ppermute | solution.py:29
  321.9 7.9 %copy-start.7 = (bf16[4,128,8,128]{3,2,1,0:T(8,128)(2,1)S(1)}, bf16[4,128,8,128]{3,2,1,0:T(8,128)(2,1)}, u32[]{:S(2)}) copy-start(bf16[4,128,8,128]{3,2,1,0:T(8,128)(2,1)} %copy.34) | copy-start | bytes 3145732
  329.8 6.0 %copy-start.4 = (f32[2,512,1024]{2,1,0:T(8,128)S(1)}, f32[2,512,1024]{2,1,0:T(8,128)}, u32[]{:S(2)}) copy-start(f32[2,512,1024]{2,1,0:T(8,128)} %slice.163) | copy-start | bytes 12582916
  335.8 62.6 %copy-start.1 = (bf16[1,512,2048]{2,1,0:T(8,128)(2,1)S(1)}, bf16[1,512,2048]{2,1,0:T(8,128)(2,1)}, u32[]{:S(2)}) copy-start(bf16[1,512,2048]{2,1,0:T(8,128)(2,1)} %param.15) | copy-start | bytes 6291460
Sparse Core Ops, SparseCore 0:
  10.8 80.8 all-gather.1
  123.3 156.2 reduce-scatter.1
  342.1 54.7 all-reduce.1
where the time goes:
time: 408 us; the launch traced here: 405 us
  local copies, waits for them, and re-layouts  168 us (41%)
  matrix products  96.1 us (24%)
  waiting for transfers between devices  62.5 us (15%)
  other arithmetic  46.3 us (11%)
  between operations  21.7 us (5%)
  starting transfers between devices  10.2 us (2%)
    dynamic_update_slice x4, local copies, waits for them, and re-layouts, advance(): lax.dynamic_update_slice_in_dim(running, current + contributions[member],...  59.1 us
    psum x1, waiting for transfers between devices, body(): summed = lax.psum(shard_sum.astype(jnp.bfloat16), 'dp').astype(jnp.float32)  51.9 us
    add x3, other arithmetic, advance(): current + contributions[member]  25.1 us
    reshape x2, local copies, waits for them, and re-layouts, advance(): contributions = jnp.stack([key_part, value_part], axis=1)  22.8 us
    gather x12, local copies, waits for them, and re-layouts  20.9 us
    dot_general x1, matrix products, advance(): jnp.einsum('jhqk,jkhd->jqhd', grad_scores, key_tiles, preferred_element_t...  19.4 us
    dot_general x1, matrix products, advance(): jnp.einsum('jhqk,jqhd->jkhd', grad_scores, query_set, preferred_element_t...  18.9 us
    gather x1, local copies, waits for them, and re-layouts, advance(): lax.dynamic_slice_in_dim(kv_source, offset, window_rows, 1)  15.4 us
  transfers between devices with their start and end apart: 7, of which 3 were waited for; matrix products, arithmetic and copies ran while one was open for 76% of the time, Pallas kernels for 0%

commit v1 on v0

--- a/solution.py
+++ b/solution.py
@@ -146,7 +146,9 @@
         scatter_dimension=0,
         tiled=True,
     )
-    summed = lax.psum(shard_sum.astype(jnp.bfloat16), "dp").astype(jnp.float32)
+    summed = jnp.sum(lax.all_gather(shard_sum.astype(jnp.bfloat16), "dp"), axis=0).astype(
+        jnp.float32
+    )
     weight_grad = summed / normalizer
     return (layer_out[None], grad_query[None], key_grad[None], value_grad[None], weight_grad)
 

time: 408 us -> 374 us (0.917)
  the two profiles are of different devices: /device:TPU:8 before, /device:TPU:128 now
where the time goes in v1:
time: 374 us; the launch traced here: 370 us
  local copies, waits for them, and re-layouts  166 us (44%)
  matrix products  96.3 us (26%)
  other arithmetic  43.3 us (12%)
  between operations  22 us (6%)
  starting transfers between devices  14.8 us (4%)
  waiting for transfers between devices  14.6 us (4%)
  blocking collectives  12.9 us (3%)
    dynamic_update_slice x4, local copies, waits for them, and re-layouts, advance(): lax.dynamic_update_slice_in_dim(running, current + contributions[member],...  59 us
    add x3, other arithmetic, advance(): current + contributions[member]  24.9 us
    reshape x2, local copies, waits for them, and re-layouts, advance(): contributions = jnp.stack([key_part, value_part], axis=1)  22.9 us
    gather x12, local copies, waits for them, and re-layouts  21 us
    dot_general x1, matrix products, advance(): jnp.einsum('jhqk,jkhd->jqhd', grad_scores, key_tiles, preferred_element_t...  19.5 us
    dot_general x1, matrix products, advance(): jnp.einsum('jhqk,jqhd->jkhd', grad_scores, query_set, preferred_element_t...  19 us
    gather x1, local copies, waits for them, and re-layouts, advance(): lax.dynamic_slice_in_dim(kv_source, offset, window_rows, 1)  15 us
    sub x1, matrix products, advance(): raised = jnp.where(inside, jnp.exp(scores - highest), 0.0)  14 us
  transfers between devices with their start and end apart: 6, of which 2 were waited for; matrix products, arithmetic and copies ran while one was open for 82% of the time, Pallas kernels for 0%

profile of v1, /device:TPU:128, one launch (start us, length us, event | category | flops | bytes accessed | tf_op | source)
XLA Modules:
  0.0 370.2 jit_solution(17527883388978645644)
XLA Ops:
  10.6 1.3 copy-done.5
  11.9 1.5 fusion.76
  13.4 3.9 %collective-permute-start.1 = (bf16[2,256,1024]{2,1,0:T(8,128)(2,1)}, bf16[2,256,1024]{2,1,0:T(8,128)(2,1)}, u32[]{:S(2)}, u32[]{:S(2)}) collective-permute-start(bf16[2,256,1024]{2,1,0:T(8,128)(2,1)} %get-tuple-element.91), channel_id=1, source_target_pairs={{4,0},{8,4},{12,8},{16,12},{20,16},{24,20},{28,24},{32,28},{36,32}... | collective-permute-start | bytes 3145736 | tf_op jit(solution)/shard_map/ppermute | solution.py:21
  17.3 1.9 collective-permute-start
  21.3 1.5 copy.54
  22.8 1.5 copy.42
  24.4 6.1 %collective-permute-done.1 = bf16[2,256,1024]{2,1,0:T(8,128)(2,1)} collective-permute-done((bf16[2,256,1024]{2,1,0:T(8,128)(2,1)}, bf16[2,256,1024]{2,1,0:T(8,128)(2,1)}, u32[]{:S(2)}, u32[]{:S(2)}) %collective-permute-start.1) | collective-permute-done | bytes 1048608 | tf_op jit(solution)/shard_map/ppermute | solution.py:21
  30.4 7.8 %collective-permute-done = bf16[2,256,1024]{2,1,0:T(8,128)(2,1)} collective-permute-done((bf16[2,256,1024]{2,1,0:T(8,128)(2,1)}, bf16[2,256,1024]{2,1,0:T(8,128)(2,1)}, u32[]{:S(2)}, u32[]{:S(2)}) %collective-permute-start) | collective-permute-done | bytes 1048608 | tf_op jit(solution)/shard_map/ppermute | solution.py:18
  38.2 3.8 %pad_maximum_fusion.1 = bf16[2,1024,1024]{2,1,0:T(8,128)(2,1)} fusion(bf16[2,256,1024]{2,1,0:T(8,128)(2,1)} %collective-permute-done.1, bf16[2,512,1024]{2,1,0:T(8,128)(2,1)} %copy-done.5, bf16[2,256,1024]{2,1,0:T(8,128)(2,1)} %collective-permute-done), kind=kLoop, calls=%fused_computation.40 | loop fusion | flops 12582912 | bytes 8388608 | tf_op jit(solution)/shard_map/concatenate | solution.py:22
  42.0 21.0 %while.3 = (s32[]{:T(128)}, bf16[2,1024,1024]{2,1,0:T(8,128)(2,1)}, s32[4,3]{1,0:T(4,128)S(1)}, bf16[4,2,640,1024]{3,2,1,0:T(8,128)(2,1)}, s32[]{:T(128)}) while((s32[]{:T(128)}, bf16[2,1024,1024]{2,1,0:T(8,128)(2,1)}, s32[4,3]{1,0:T(4,128)S(1)}, bf16[4,2,640,1024]{3,2,1,0:T(8,128)(2,1)}, s32[]{:T(128)}) %tuple.39), condition=%wide.while_cond.2, body=%wide.while_body.2.sunk | while | flops 2 | bytes 5243501 | solution.py:45
  42.6 4.7 %bitcast_dynamic-update-slice_fusion.2 = bf16[4,2,640,1024]{3,2,1,0:T(8,128)(2,1)} fusion(bf16[4,2,640,1024]{3,2,1,0:T(8,128)(2,1)} %get-tuple-element.131, s32[]{:T(128)S(6)} %copy.69, bf16[2,1024,1024]{2,1,0:T(8,128)(2,1)} %get-tuple-element.134, s32[]{:T(128)} %bitcast.106), kind=kLoop, calls=%fused_computation.3.clone.1 | loop fusion | bytes 5243396 | tf_op jit(solution)/shard_map/while/body/eval_jaxpr/vmap()/gather
  47.8 4.7 %bitcast_dynamic-update-slice_fusion.2 = bf16[4,2,640,1024]{3,2,1,0:T(8,128)(2,1)} fusion(bf16[4,2,640,1024]{3,2,1,0:T(8,128)(2,1)} %get-tuple-element.131, s32[]{:T(128)S(6)} %copy.69, bf16[2,1024,1024]{2,1,0:T(8,128)(2,1)} %get-tuple-element.134, s32[]{:T(128)} %bitcast.106), kind=kLoop, calls=%fused_computation.3.clone.1 | loop fusion | bytes 5243396 | tf_op jit(solution)/shard_map/while/body/eval_jaxpr/vmap()/gather
  53.1 4.6 %bitcast_dynamic-update-slice_fusion.2 = bf16[4,2,640,1024]{3,2,1,0:T(8,128)(2,1)} fusion(bf16[4,2,640,1024]{3,2,1,0:T(8,128)(2,1)} %get-tuple-element.131, s32[]{:T(128)S(6)} %copy.69, bf16[2,1024,1024]{2,1,0:T(8,128)(2,1)} %get-tuple-element.134, s32[]{:T(128)} %bitcast.106), kind=kLoop, calls=%fused_computation.3.clone.1 | loop fusion | bytes 5243396 | tf_op jit(solution)/shard_map/while/body/eval_jaxpr/vmap()/gather
  58.3 4.7 %bitcast_dynamic-update-slice_fusion.2 = bf16[4,2,640,1024]{3,2,1,0:T(8,128)(2,1)} fusion(bf16[4,2,640,1024]{3,2,1,0:T(8,128)(2,1)} %get-tuple-element.131, s32[]{:T(128)S(6)} %copy.69, bf16[2,1024,1024]{2,1,0:T(8,128)(2,1)} %get-tuple-element.134, s32[]{:T(128)} %bitcast.106), kind=kLoop, calls=%fused_computation.3.clone.1 | loop fusion | bytes 5243396 | tf_op jit(solution)/shard_map/while/body/eval_jaxpr/vmap()/gather
  63.0 5.5 %slice.116 = bf16[4,1,640,1024]{3,2,1,0:T(8,128)(2,1)} slice(bf16[4,2,640,1024]{3,2,1,0:T(8,128)(2,1)} %get-tuple-element.69), slice={[0:4], [1:2], [0:640], [0:1024]} | slice | bytes 10485760 | tf_op jit(solution)/shard_map/while/body/eval_jaxpr/slice | solution.py:48
  68.5 15.0 %copy.30 = bf16[4,2,640,1024]{2,3,0,1:T(8,128)(2,1)} copy(bf16[4,2,640,1024]{3,2,1,0:T(8,128)(2,1)} %get-tuple-element.69) | data formatting | bytes 20971520 | tf_op jit(solution)/shard_map/while/body/eval_jaxpr/vmap()/gather | solution.py:45
  83.4 8.0 %copy.29 = bf16[4,1,640,1024]{2,3,0,1:T(8,128)(2,1)} copy(bf16[4,1,640,1024]{3,2,1,0:T(8,128)(2,1)} %slice.116) | data formatting | bytes 10485760 | tf_op jit(solution)/shard_map/while/body/eval_jaxpr/slice | solution.py:48
  91.5 5.3 %slice.156 = bf16[4,1,640,1024]{2,3,0,1:T(8,128)(2,1)} slice(bf16[4,2,640,1024]{2,3,0,1:T(8,128)(2,1)} %copy.30), slice={[0:4], [0:1], [0:640], [0:1024]} | slice | bytes 10485760 | tf_op jit(solution)/shard_map/while/body/eval_jaxpr/slice | solution.py:47
  96.8 14.0 %bitcast_reduce_fusion = (f32[4,8,128]{2,1,0:T(8,128)S(1)}, f32[4,8,640,128]{3,2,1,0:T(8,128)}) fusion(pred[4,640]{1,0:T(4,128)(4,1)S(1)} %compare_and_fusion, bf16[4,640,8,128]{1,3,2,0:T(8,128)(2,1)} %bitcast.113, bf16[4,128,8,128]{1,3,2,0:T(8,128)(2,1)S(1)} %copy-done.6), kind=kOutput, calls=%fused_computation.14 | convolution fusion | flops 1357906560 | bytes 16796160 | tf_op jit(solution)/shard_map/while/body/eval_jaxpr/sub | solution.py:61
  110.8 8.0 %fusion.50 = bf16[4,128,8,128]{1,3,2,0:T(8,128)(2,1)} fusion(bf16[4,640,8,128]{1,3,2,0:T(8,128)(2,1)} %bitcast.109, f32[4,8,640,128]{3,2,1,0:T(8,128)} %get-tuple-element.97, f32[4,8,128]{2,1,0:T(8,128)S(1)} %get-tuple-element.96), kind=kOutput, calls=%fused_computation.58 | convolution fusion | flops 676855808 | bytes 16793600 | tf_op jit(solution)/shard_map/while/body/eval_jaxpr/jhqk,jkhd->jqhd/dot_general | solution.py:64
  118.8 2.4 copy.34
  121.2 7.0 %fusion.37 = f32[1024,2048]{1,0:T(8,128)} fusion(bf16[1,512,2048]{2,1,0:T(8,128)(2,1)S(1)} %copy-done, bf16[64,8,8,128]{3,2,1,0:T(8,128)(2,1)} %bitcast.119), kind=kOutput, calls=%fused_computation.51 | convolution fusion | flops 2147483648 | bytes 11534336 | tf_op jit(solution)/shard_map/dot_general | solution.py:142
  136.6 4.6 %fusion.56 = bf16[64,8,8,128]{3,1,2,0:T(8,128)(2,1)S(1)} fusion(bf16[1024,2048]{1,0:T(8,128)(2,1)} %all-gather.3.cloned.1.call-done, bf16[1,512,2048]{2,1,0:T(8,128)(2,1)S(1)} %copy-done), kind=kOutput, calls=%fused_computation.60 | convolution fusion | flops 2148007936 | bytes 7340032 | tf_op jit(solution)/shard_map/dot_general | solution.py:111
  142.3 8.0 %fusion.78 = f32[4,8,128,640]{2,3,1,0:T(8,128)} fusion(bf16[4,128,8,128]{1,3,2,0:T(8,128)(2,1)S(1)} %copy.43, bf16[4,640,8,128]{1,3,2,0:T(8,128)(2,1)} %bitcast.110), kind=kOutput, calls=%fused_computation.94 | convolution fusion | flops 671088640 | bytes 16777216 | tf_op jit(solution)/shard_map/while/body/eval_jaxpr/jqhd,jkhd->jhqk/dot_general | solution.py:67
  150.3 19.0 %fusion.10 = f32[4,8,640,128]{2,3,1,0:T(8,128)} fusion(bf16[4,128,8,128]{1,3,2,0:T(8,128)(2,1)S(1)} %copy-done.6, f32[4,8,128,640]{2,3,1,0:T(8,128)} %fusion.78, f32[4,8,640,128]{3,2,1,0:T(8,128)} %get-tuple-element.97, f32[4,8,128]{2,1,0:T(8,128)S(1)} %get-tuple-element.96), kind=kOutput, calls=%fused_computation.22 | convolution fusion | flops 689443456 | bytes 32522240 | tf_op jit(solution)/shard_map/while/body/eval_jaxpr/jhqk,jqhd->jkhd/dot_general | solution.py:75
  169.3 11.5 %copy.45 = f32[4,1,640,1024]{3,2,1,0:T(8,128)} copy(f32[4,1,640,1024]{2,3,0,1:T(8,128)} %bitcast.111) | data formatting | bytes 20971520 | tf_op jit(solution)/shard_map/while/body/eval_jaxpr/stack;while/body/eval_jaxpr/reshape | solution.py:81
  180.9 10.2 %fusion.31 = f32[4,8,128,640]{3,2,1,0:T(8,128)} fusion(bf16[4,128,8,128]{1,3,2,0:T(8,128)(2,1)S(1)} %copy.43, f32[4,8,640,128]{3,2,1,0:T(8,128)} %get-tuple-element.97, f32[4,8,128]{2,1,0:T(8,128)S(1)} %get-tuple-element.96), kind=kOutput, calls=%fused_computation.43 | convolution fusion | flops 676331520 | bytes 22036480 | tf_op jit(solution)/shard_map/while/body/eval_jaxpr/jhqk,jqhd->jkhd/dot_general | solution.py:78
  191.0 11.3 %copy.46 = f32[4,1,640,1024]{3,2,1,0:T(8,128)} copy(f32[4,1,640,1024]{2,3,0,1:T(8,128)} %bitcast.112) | data formatting | bytes 20971520 | tf_op jit(solution)/shard_map/while/body/eval_jaxpr/stack;while/body/eval_jaxpr/reshape | solution.py:81
  202.4 5.7 %fusion.19 = f32[2,640,1024]{2,1,0:T(8,128)} fusion(f32[4,1,640,1024]{3,2,1,0:T(8,128)} %copy.45, f32[4,1,640,1024]{3,2,1,0:T(8,128)} %copy.46), kind=kLoop, calls=%fused_computation.28 | loop fusion | flops 1310720 | bytes 26214400 | tf_op jit(solution)/shard_map/while/body/eval_jaxpr/squeeze | solution.py:86
  208.1 4.3 %broadcast_in_dim.65 = f32[2,1024,1024]{2,1,0:T(8,128)} broadcast(f32[]{:T(128)} %constant.120.clone.1), dimensions={} | broadcast | bytes 8388612 | tf_op jit(solution)/shard_map/broadcast_in_dim | solution.py:93
  212.3 15.0 %dynamic_update_slice.21 = f32[2,1024,1024]{2,1,0:T(8,128)} dynamic-update-slice(f32[2,1024,1024]{2,1,0:T(8,128)} %broadcast_in_dim.65, f32[2,640,1024]{2,1,0:T(8,128)} %fusion.19, s32[]{:T(128)} %constant.107.clone.1, s32[]{:T(128)S(6)} %select_n.64, s32[]{:T(128)} %constant.107.clone.1) | dynamic-update-slice | bytes 10485764 | tf_op jit(solution)/shard_map/while/body/eval_jaxpr/dynamic_update_slice | solution.py:85
  227.3 8.3 %fusion.22 = f32[2,640,1024]{2,1,0:T(8,128)} fusion(f32[4,1,640,1024]{3,2,1,0:T(8,128)} %copy.45, f32[4,1,640,1024]{3,2,1,0:T(8,128)} %copy.46, f32[2,1024,1024]{2,1,0:T(8,128)} %dynamic_update_slice.21, s32[]{:T(128)S(6)} %select_n.65), kind=kLoop, calls=%fused_computation.31 | loop fusion | flops 2621440 | bytes 31457284 | tf_op jit(solution)/shard_map/while/body/eval_jaxpr/add | solution.py:86
  235.6 14.9 %dynamic_update_slice.22 = f32[2,1024,1024]{2,1,0:T(8,128)} dynamic-update-slice(f32[2,1024,1024]{2,1,0:T(8,128)} %dynamic_update_slice.21, f32[2,640,1024]{2,1,0:T(8,128)} %fusion.22, s32[]{:T(128)} %constant.107.clone.1, s32[]{:T(128)S(6)} %select_n.65, s32[]{:T(128)} %constant.107.clone.1) | dynamic-update-slice | bytes 10485764 | tf_op jit(solution)/shard_map/while/body/eval_jaxpr/dynamic_update_slice | solution.py:85
  250.5 8.3 %fusion.17 = f32[2,640,1024]{2,1,0:T(8,128)} fusion(f32[4,1,640,1024]{3,2,1,0:T(8,128)} %copy.45, f32[4,1,640,1024]{3,2,1,0:T(8,128)} %copy.46, f32[2,1024,1024]{2,1,0:T(8,128)} %dynamic_update_slice.22, s32[]{:T(128)S(6)} %select_n.66), kind=kLoop, calls=%fused_computation.26 | loop fusion | flops 2621440 | bytes 31457284 | tf_op jit(solution)/shard_map/while/body/eval_jaxpr/add | solution.py:86
  258.8 14.9 %dynamic_update_slice.23 = f32[2,1024,1024]{2,1,0:T(8,128)} dynamic-update-slice(f32[2,1024,1024]{2,1,0:T(8,128)} %dynamic_update_slice.22, f32[2,640,1024]{2,1,0:T(8,128)} %fusion.17, s32[]{:T(128)} %constant.107.clone.1, s32[]{:T(128)S(6)} %select_n.66, s32[]{:T(128)} %constant.107.clone.1) | dynamic-update-slice | bytes 10485764 | tf_op jit(solution)/shard_map/while/body/eval_jaxpr/dynamic_update_slice | solution.py:85
  273.7 8.3 %fusion.24 = f32[2,640,1024]{2,1,0:T(8,128)} fusion(f32[4,1,640,1024]{3,2,1,0:T(8,128)} %copy.46, f32[4,1,640,1024]{3,2,1,0:T(8,128)} %copy.45, f32[2,1024,1024]{2,1,0:T(8,128)} %dynamic_update_slice.23, s32[]{:T(128)S(6)} %select_n.67), kind=kLoop, calls=%fused_computation.34 | loop fusion | flops 2621440 | bytes 31457284 | tf_op jit(solution)/shard_map/while/body/eval_jaxpr/add | solution.py:86
  282.0 14.3 %dynamic_update_slice.24 = f32[2,1024,1024]{2,1,0:T(8,128)} dynamic-update-slice(f32[2,1024,1024]{2,1,0:T(8,128)} %dynamic_update_slice.23, f32[2,640,1024]{2,1,0:T(8,128)} %fusion.24, s32[]{:T(128)} %constant.107.clone.1, s32[]{:T(128)S(6)} %select_n.67, s32[]{:T(128)} %constant.107.clone.1) | dynamic-update-slice | bytes 10485764 | tf_op jit(solution)/shard_map/while/body/eval_jaxpr/dynamic_update_slice | solution.py:85
  296.2 4.0 %convert.9 = bf16[2,1024,1024]{2,1,0:T(8,128)(2,1)S(1)} convert(f32[2,1024,1024]{2,1,0:T(8,128)} %dynamic_update_slice.24) | non-fusion elementwise | flops 2097152 | bytes 12582912 | tf_op jit(solution)/shard_map/convert.4
  300.3 1.5 fusion.74
  301.8 1.9 collective-permute-start.2
  303.7 7.0 %collective-permute-start.3 = (bf16[2,256,1024]{2,1,0:T(8,128)(2,1)}, bf16[2,256,1024]{2,1,0:T(8,128)(2,1)S(1)}, u32[]{:S(2)}, u32[]{:S(2)}) collective-permute-start(bf16[2,256,1024]{2,1,0:T(8,128)(2,1)} %get-tuple-element.86), channel_id=1, source_target_pairs={{4,0},{8,4},{12,8},{16,12},{20,16},{24,20},{28,24},{32,28},{36,32}... | collective-permute-start | bytes 3145736 | tf_op jit(solution)/shard_map/ppermute | solution.py:29
  310.7 19.5 %fusion.53 = bf16[4,128,8,128]{1,3,2,0:T(8,128)(2,1)} fusion(bf16[4,640,8,128]{1,3,2,0:T(8,128)(2,1)} %bitcast.114, f32[4,8,128,640]{2,3,1,0:T(8,128)} %fusion.78, f32[4,8,640,128]{3,2,1,0:T(8,128)} %get-tuple-element.97, f32[4,8,128]{2,1,0:T(8,128)S(1)} %get-tuple-element.96), kind=kOutput, calls=%fused_computation.59 | convolution fusion | flops 689967744 | bytes 27279360 | tf_op jit(solution)/shard_map/while/body/eval_jaxpr/jhqk,jkhd->jqhd/dot_general | solution.py:72
  330.2 4.9 %slice.163 = f32[2,512,1024]{2,1,0:T(8,128)} slice(f32[2,1024,1024]{2,1,0:T(8,128)} %dynamic_update_slice.24), slice={[0:2], [256:768], [0:1024]} | slice | bytes 8388608 | tf_op jit(solution)/shard_map/slice | solution.py:132
  335.1 1.7 copy.40
  338.1 6.0 %fusion.30 = bf16[1,512,2048]{2,1,0:T(8,128)(2,1)} fusion(bf16[1024,2048]{1,0:T(8,128)(2,1)} %all-gather.3.cloned.1.call-done, bf16[64,8,8,128]{3,2,1,0:T(8,128)(2,1)S(1)} %bitcast.120), kind=kOutput, calls=%fused_computation.42 | convolution fusion | flops 2148532224 | bytes 7340032 | tf_op jit(solution)/shard_map/dot_general | solution.py:137
  344.1 2.3 fusion.36
  347.3 1.5 fusion.75
  349.7 12.9 %all-gather = bf16[64,2048]{1,0:T(8,128)(2,1)S(1)} all-gather(bf16[16,2048]{1,0:T(8,128)(2,1)S(1)} %convert_element_type.58), channel_id=2, replica_groups=mesh['seq'=64,'dp'=4] {'dp'}, dimensions={0}, use_global_device_ids=true | all-gather | bytes 327680 | tf_op jit(solution)/shard_map/all_gather | solution.py:149
  (55 shorter events, 13.4 us)
Async XLA Ops:
  7.2 114.1 %copy-start = (bf16[1,512,2048]{2,1,0:T(8,128)(2,1)S(1)}, bf16[1,512,2048]{2,1,0:T(8,128)(2,1)}, u32[]{:S(2)}) copy-start(bf16[1,512,2048]{2,1,0:T(8,128)(2,1)} %param.15) | copy-start | bytes 6291460
  7.2 12.8 %copy-start.2 = (s32[1,4]{1,0:T(1,128)S(1)}, s32[1,4]{1,0:T(1,128)}, u32[]{:S(2)}) copy-start(s32[1,4]{1,0:T(1,128)} %param.17) | copy-start | bytes 52
  7.2 13.5 %copy-start.3 = (s32[1,4]{1,0:T(1,128)S(1)}, s32[1,4]{1,0:T(1,128)}, u32[]{:S(2)}) copy-start(s32[1,4]{1,0:T(1,128)} %param.16) | copy-start | bytes 52
  7.2 129.4 %all-gather.3.cloned.1.call-start = ((), (), s32[]{:S(2)}) async-start(), calls=%async_computation.1 | async-start | bytes 4259840 | tf_op jit(solution)/shard_map/all_gather | solution.py:110
  7.9 340.9 %reduce-scatter.2.cloned.1.call-start = ((), (), s32[]{:S(2)}) async-start(), calls=%async_computation.2 | async-start | bytes 8519680 | tf_op jit(solution)/shard_map/reduce_scatter | solution.py:141
  10.6 1.3 copy-start.5
  13.4 17.0 %collective-permute-start.1 = (bf16[2,256,1024]{2,1,0:T(8,128)(2,1)}, bf16[2,256,1024]{2,1,0:T(8,128)(2,1)}, u32[]{:S(2)}, u32[]{:S(2)}) collective-permute-start(bf16[2,256,1024]{2,1,0:T(8,128)(2,1)} %get-tuple-element.91), channel_id=1, source_target_pairs={{4,0},{8,4},{12,8},{16,12},{20,16},{24,20},{28,24},{32,28},{36,32}... | collective-permute-start | bytes 3145736 | tf_op jit(solution)/shard_map/ppermute | solution.py:21
  17.3 20.9 %collective-permute-start = (bf16[2,256,1024]{2,1,0:T(8,128)(2,1)}, bf16[2,256,1024]{2,1,0:T(8,128)(2,1)}, u32[]{:S(2)}, u32[]{:S(2)}) collective-permute-start(bf16[2,256,1024]{2,1,0:T(8,128)(2,1)} %get-tuple-element.90), channel_id=1, source_target_pairs={{0,4},{4,8},{8,12},{12,16},{16,20},{20,24},{24,28},{28,32},{32,36}... | collective-permute-start | bytes 3145736 | tf_op jit(solution)/shard_map/ppermute | solution.py:18
  83.4 13.3 %copy-start.6 = (bf16[4,128,8,128]{1,3,2,0:T(8,128)(2,1)S(1)}, bf16[4,128,8,128]{1,3,2,0:T(8,128)(2,1)}, u32[]{:S(2)}) copy-start(bf16[4,128,8,128]{1,3,2,0:T(8,128)(2,1)} %copy.42) | copy-start | bytes 3145732
  301.8 42.2 %collective-permute-start.2 = (bf16[2,256,1024]{2,1,0:T(8,128)(2,1)}, bf16[2,256,1024]{2,1,0:T(8,128)(2,1)}, u32[]{:S(2)}, u32[]{:S(2)}) collective-permute-start(bf16[2,256,1024]{2,1,0:T(8,128)(2,1)} %get-tuple-element.87), channel_id=1, source_target_pairs={{0,4},{4,8},{8,12},{12,16},{16,20},{20,24},{24,28},{28,32},{32,36}... | collective-permute-start | bytes 3145736 | tf_op jit(solution)/shard_map/ppermute | solution.py:29
  303.7 42.6 %collective-permute-start.3 = (bf16[2,256,1024]{2,1,0:T(8,128)(2,1)}, bf16[2,256,1024]{2,1,0:T(8,128)(2,1)S(1)}, u32[]{:S(2)}, u32[]{:S(2)}) collective-permute-start(bf16[2,256,1024]{2,1,0:T(8,128)(2,1)} %get-tuple-element.86), channel_id=1, source_target_pairs={{4,0},{8,4},{12,8},{16,12},{20,16},{24,20},{28,24},{32,28},{36,32}... | collective-permute-start | bytes 3145736 | tf_op jit(solution)/shard_map/ppermute | solution.py:29
  330.2 7.9 %copy-start.7 = (bf16[4,128,8,128]{3,2,1,0:T(8,128)(2,1)S(1)}, bf16[4,128,8,128]{3,2,1,0:T(8,128)(2,1)}, u32[]{:S(2)}) copy-start(bf16[4,128,8,128]{3,2,1,0:T(8,128)(2,1)} %copy.34) | copy-start | bytes 3145732
  338.0 6.0 %copy-start.4 = (f32[2,512,1024]{2,1,0:T(8,128)S(1)}, f32[2,512,1024]{2,1,0:T(8,128)}, u32[]{:S(2)}) copy-start(f32[2,512,1024]{2,1,0:T(8,128)} %slice.163) | copy-start | bytes 12582916
  344.1 19.3 %copy-start.1 = (bf16[1,512,2048]{2,1,0:T(8,128)(2,1)S(1)}, bf16[1,512,2048]{2,1,0:T(8,128)(2,1)}, u32[]{:S(2)}) copy-start(bf16[1,512,2048]{2,1,0:T(8,128)(2,1)} %param.15) | copy-start | bytes 6291460
Sparse Core Ops, SparseCore 0:
  10.8 78.0 all-gather.2
  128.3 148.9 reduce-scatter.1
